TPU v7x, 128 devices: a whole 4x4x4 slice. The times are simulated.
128 devices in a mesh: row: 4 (over x), col: 32 (over z, y, core).
Axes of the slice: x: 4, y: 4, z: 4, core: 2. Of those that a mesh axis runs over, the one named last changes fastest.
Arguments:
- tokens: bfloat16 [512, 8192], P('col', 'row'), may hold values from -6 to 6
- out_grad: bfloat16 [512, 8192], P('col', 'row'), may hold values from -6 to 6
- gate_weight: bfloat16 [8192, 29568], P('row', 'col'), may hold values from -0.0625 to 0.0625
- up_weight: bfloat16 [8192, 29568], P('row', 'col'), may hold values from -0.0625 to 0.0625
- down_weight: bfloat16 [29568, 8192], P('col', 'row'), may hold values from -0.03125 to 0.03125
Outputs:
- input_grad: bfloat16 [512, 8192], P('col', 'row')
- gate_wgrad: bfloat16 [8192, 29568], P('row', 'col')
- up_wgrad: bfloat16 [8192, 29568], P('row', 'col')
- down_wgrad: bfloat16 [29568, 8192], P('col', 'row')
All inputs are finite; a program needn't handle non-finite values.
Results may differ from a plain program's by a relative error of at most 0.005.
Values may be sent and summed in bfloat16 or wider, within the bound.
No kernel may reach another device: no remote copies, remote signals or barrier semaphores. Data moves between devices by JAX's collectives and lax.ppermute only.
A program may use at most 128 MiB of HBM per device.

v0:
```python
import math
import jax
import jax.numpy as jnp
from jax import lax
from jax.sharding import PartitionSpec as P


def contract(left, right, left_dim, right_dim):
    return lax.dot_general(
        left, right, (((left_dim,), (right_dim,)), ((), ())), preferred_element_type=jnp.float32
    )


def swiglu_backward(gate, upward, hid_grad):
    sig = jax.nn.sigmoid(gate)
    act = gate * sig
    hidden = (act * upward).astype(jnp.bfloat16)
    gate_grad = (hid_grad * upward * sig * (1.0 + gate * (1.0 - sig))).astype(jnp.bfloat16)
    up_grad = (hid_grad * act).astype(jnp.bfloat16)
    return (hidden, gate_grad, up_grad)


def local(tokens, out_grad, gate_weight, up_weight, down_weight):
    panel_tokens, panel_grads = (
        lax.all_gather(tokens, "col", axis=0, tiled=True),
        lax.all_gather(out_grad, "col", axis=0, tiled=True),
    )
    factor = 1.0 / math.sqrt(panel_tokens.shape[0])
    gate_part = jnp.dot(panel_tokens, gate_weight, preferred_element_type=jnp.float32)
    up_part = jnp.dot(panel_tokens, up_weight, preferred_element_type=jnp.float32)
    grad_part = contract(panel_grads, down_weight, 1, 1)
    gate, upward, hid_grad = lax.psum((gate_part, up_part, grad_part), "row")
    hidden, gate_grad, up_grad = swiglu_backward(gate, upward, hid_grad)
    input_grad = lax.psum_scatter(
        contract(gate_grad, gate_weight, 1, 1) + contract(up_grad, up_weight, 1, 1),
        "col",
        scatter_dimension=0,
        tiled=True,
    ).astype(jnp.bfloat16)
    gate_wgrad = (contract(panel_tokens, gate_grad, 0, 0) * factor).astype(jnp.bfloat16)
    up_wgrad = (contract(panel_tokens, up_grad, 0, 0) * factor).astype(jnp.bfloat16)
    down_wgrad = (contract(hidden, panel_grads, 0, 0) * factor).astype(jnp.bfloat16)
    return (input_grad, gate_wgrad, up_wgrad, down_wgrad)


def solution(mesh):
    placed = (P("col", "row"), P("col", "row"), P("row", "col"), P("row", "col"), P("col", "row"))
    return jax.shard_map(
        local,
        mesh=mesh,
        in_specs=placed,
        out_specs=(P("col", "row"), P("row", "col"), P("row", "col"), P("col", "row")),
        check_vma=False,
    )
```

profile of v0, /device:TPU:0, one launch (start us, length us, event | category | flops | bytes accessed | tf_op | source)
XLA Modules:
  0.0 326.6 jit_solution(14472059379591102396)
XLA Ops:
  7.2 0.0 all-gather.5.cloned.1.call-start
  7.2 0.7 all-gather.5.cloned.1.call-update
  7.9 0.0 all-gather.3.cloned.1.call-start
  7.9 0.7 all-gather.3.cloned.1.call-update
  8.6 0.0 all-reduce.3.cloned.1.call-start
  8.7 48.1 %all-gather.5.cloned.1.call-done = bf16[512,2048]{1,0:T(8,128)(2,1)} async-done(((bf16[16,2048]{1,0:T(8,128)(2,1)}), bf16[512,2048]{1,0:T(8,128)(2,1)}) %all-gather.5.cloned.1.call-update) | async-done | bytes 2097168 | tf_op jit(solution)/shard_map/all_gather | solution.py:25
  56.8 6.3 %fusion.6 = f32[512,924]{0,1:T(8,128)} fusion(bf16[512,2048]{1,0:T(8,128)(2,1)} %all-gather.5.cloned.1.call-done, bf16[2048,924]{0,1:T(8,128)(2,1)} %param.8), kind=kOutput, calls=%fused_computation.13 | convolution fusion | flops 1937768448 | bytes 7774208 | tf_op jit(solution)/shard_map/dot_general | solution.py:30
  63.0 0.0 copy-done
  63.0 0.0 copy-done.5
  63.0 3.4 %fusion.7 = f32[512,924]{0,1:T(8,128)} fusion(bf16[512,2048]{1,0:T(8,128)(2,1)S(1)} %copy-done.5, bf16[2048,924]{0,1:T(8,128)(2,1)S(1)} %copy-done), kind=kOutput, calls=%fused_computation.14 | convolution fusion | flops 1937768448 | bytes 7774208 | tf_op jit(solution)/shard_map/dot_general | solution.py:29
  66.4 35.8 %all-gather.3.cloned.1.call-done = bf16[512,2048]{1,0:T(8,128)(2,1)} async-done(((bf16[16,2048]{1,0:T(8,128)(2,1)}), bf16[512,2048]{1,0:T(8,128)(2,1)}) %all-gather.3.cloned.1.call-update) | async-done | bytes 2097168 | tf_op jit(solution)/shard_map/all_gather | solution.py:26
  102.3 6.1 %fusion.5 = f32[512,924]{0,1:T(8,128)} fusion(bf16[512,2048]{1,0:T(8,128)(2,1)} %all-gather.3.cloned.1.call-done, bf16[924,2048]{1,0:T(8,128)(2,1)} %param.9), kind=kOutput, calls=%fused_computation.12 | convolution fusion | flops 1937768448 | bytes 7774208 | tf_op jit(solution)/shard_map/dot_general | solution.py:9
  108.4 0.0 all-reduce.3.cloned.1.call-update
  108.4 0.2 reduce-scatter.2.cloned.1.call-start
  108.7 116.8 %all-reduce.3.cloned.1.call-done = (f32[512,924]{0,1:T(8,128)}, f32[512,924]{0,1:T(8,128)}, f32[512,924]{0,1:T(8,128)}) async-done(((f32[512,924]{0,1:T(8,128)}, f32[512,924]{0,1:T(8,128)}, f32[512,924]{0,1:T(8,128)}), (f32[512,924]{0,1:T(8,128)}, f32[512,924]{0,1:T(8,128)}, f32[512,924]{0,1:T(8,128)})) %all-reduce.3.cloned.1.call-update) | async-done | bytes 5677072 | tf_op jit(solution)/shard_map/psum | solution.py:32
  225.4 3.9 %multiply_convert_fusion.4 = (bf16[512,924]{0,1:T(8,128)(2,1)S(1)}, bf16[512,924]{0,1:T(8,128)(2,1)S(1)}) fusion(f32[512,924]{0,1:T(8,128)} %get-tuple-element.5, f32[512,924]{0,1:T(8,128)} %get-tuple-element.4, f32[512,924]{0,1:T(8,128)} %get-tuple-element.6), kind=kLoop, calls=%fused_computation.7 | loop fusion | flops 6150144 | bytes 7569408 | tf_op jit(solution)/shard_map/convert_element_type | solution.py:19
  229.3 0.0 copy-done.1
  229.3 0.0 copy-start.2
  229.3 2.4 fusion.8
  231.8 0.0 copy-done.2
  231.8 4.5 %convolution_add_fusion = f32[512,2048]{1,0:T(8,128)} fusion(f32[512,2048]{1,0:T(8,128)S(1)} %fusion.8, bf16[512,924]{0,1:T(8,128)(2,1)S(1)} %get-tuple-element.7, bf16[2048,924]{0,1:T(8,128)(2,1)S(1)} %copy-done.2), kind=kOutput, calls=%fused_computation.5 | convolution fusion | flops 1938817024 | bytes 13119488 | tf_op jit(solution)/shard_map/dot_general | solution.py:9
  236.3 0.0 reduce-scatter.2.cloned.1.call-update
  236.3 0.0 copy-start.6
  236.3 5.8 %fusion = bf16[2048,924]{0,1:T(8,128)(2,1)} fusion(bf16[512,924]{0,1:T(8,128)(2,1)S(1)} %get-tuple-element.8, bf16[512,2048]{1,0:T(8,128)(2,1)} %all-gather.5.cloned.1.call-done), kind=kOutput, calls=%fused_computation.3 | convolution fusion | flops 1941553152 | bytes 6828032 | tf_op jit(solution)/shard_map/dot_general | solution.py:9
  242.1 0.0 copy-done.6
  242.1 4.1 %fusion.1 = bf16[2048,924]{0,1:T(8,128)(2,1)} fusion(bf16[512,924]{0,1:T(8,128)(2,1)S(1)} %get-tuple-element.7, bf16[512,2048]{1,0:T(8,128)(2,1)S(1)} %copy-done.6), kind=kOutput, calls=%fused_computation.4 | convolution fusion | flops 1941553152 | bytes 6828032 | tf_op jit(solution)/shard_map/dot_general | solution.py:9
  246.2 0.0 copy-done.3
  246.2 0.0 copy-done.4
  246.2 0.0 copy-done.7
  246.2 4.1 %multiply_convert_fusion = bf16[924,2048]{1,0:T(8,128)(2,1)} fusion(bf16[512,2048]{1,0:T(8,128)(2,1)S(1)} %copy-done.7, f32[512,924]{0,1:T(8,128)S(1)} %copy-done.4, f32[512,924]{0,1:T(8,128)S(1)} %copy-done.3), kind=kOutput, calls=%fused_computation | convolution fusion | flops 1944391680 | bytes 9666560 | tf_op jit(solution)/shard_map/dot_general | solution.py:9
  250.3 68.2 %reduce-scatter.2.cloned.1.call-done = f32[16,2048]{1,0:T(8,128)} async-done(((f32[512,2048]{1,0:T(8,128)}), f32[16,2048]{1,0:T(8,128)}) %reduce-scatter.2.cloned.1.call-update) | async-done | bytes 131088 | tf_op jit(solution)/shard_map/reduce_scatter | solution.py:34
  318.5 1.5 convert_element_type.29
  (6 shorter events, 0.0 us)
Async XLA Ops:
  7.2 49.6 %all-gather.5.cloned.1.call-start = ((), (), s32[]{:S(2)}) async-start(), calls=%async_computation.2 | async-start | bytes 2162688 | tf_op jit(solution)/shard_map/all_gather | solution.py:25
  7.9 94.4 %all-gather.3.cloned.1.call-start = ((), (), s32[]{:S(2)}) async-start(), calls=%async_computation.1 | async-start | bytes 2162688 | tf_op jit(solution)/shard_map/all_gather | solution.py:26
  8.6 216.8 %all-reduce.3.cloned.1.call-start = ((), (), s32[]{:S(2)}) async-start(), calls=%async_computation.4 | async-start | bytes 11403264 | tf_op jit(solution)/shard_map/psum | solution.py:32
  56.8 6.3 %copy-start = (bf16[2048,924]{0,1:T(8,128)(2,1)S(1)}, bf16[2048,924]{0,1:T(8,128)(2,1)}, u32[]{:S(2)}) copy-start(bf16[2048,924]{0,1:T(8,128)(2,1)} %param.7) | copy-start | bytes 11354116
  56.8 6.3 %copy-start.5 = (bf16[512,2048]{1,0:T(8,128)(2,1)S(1)}, bf16[512,2048]{1,0:T(8,128)(2,1)}, u32[]{:S(2)}) copy-start(bf16[512,2048]{1,0:T(8,128)(2,1)} %all-gather.5.cloned.1.call-done) | copy-start | bytes 6291460
  108.4 210.1 %reduce-scatter.2.cloned.1.call-start = ((), (), s32[]{:S(2)}) async-start(), calls=%async_computation.3 | async-start | bytes 4325376 | tf_op jit(solution)/shard_map/reduce_scatter | solution.py:34
  225.4 3.9 %copy-start.1 = (bf16[2048,924]{0,1:T(8,128)(2,1)S(1)}, bf16[2048,924]{0,1:T(8,128)(2,1)}, u32[]{:S(2)}) copy-start(bf16[2048,924]{0,1:T(8,128)(2,1)} %param.7) | copy-start | bytes 11354116
  229.3 2.4 copy-start.2
  236.3 5.8 %copy-start.6 = (bf16[512,2048]{1,0:T(8,128)(2,1)S(1)}, bf16[512,2048]{1,0:T(8,128)(2,1)}, u32[]{:S(2)}) copy-start(bf16[512,2048]{1,0:T(8,128)(2,1)} %all-gather.5.cloned.1.call-done) | copy-start | bytes 6291460
  242.1 4.1 %copy-start.3 = (f32[512,924]{0,1:T(8,128)S(1)}, f32[512,924]{0,1:T(8,128)}, u32[]{:S(2)}) copy-start(f32[512,924]{0,1:T(8,128)} %get-tuple-element.4) | copy-start | bytes 5677060
  242.1 4.1 %copy-start.4 = (f32[512,924]{0,1:T(8,128)S(1)}, f32[512,924]{0,1:T(8,128)}, u32[]{:S(2)}) copy-start(f32[512,924]{0,1:T(8,128)} %get-tuple-element.6) | copy-start | bytes 5677060
  242.1 4.1 %copy-start.7 = (bf16[512,2048]{1,0:T(8,128)(2,1)S(1)}, bf16[512,2048]{1,0:T(8,128)(2,1)}, u32[]{:S(2)}) copy-start(bf16[512,2048]{1,0:T(8,128)(2,1)} %all-gather.3.cloned.1.call-done) | copy-start | bytes 6291460
Sparse Core Ops, SparseCore 0:
  10.3 46.4 all-gather.4
  59.0 43.2 all-gather.2
  108.5 116.8 all-reduce.2
  236.4 81.9 reduce-scatter.1
where the time goes:
time: 327 us
  waiting for transfers between devices  270 us (83%)
  matrix products  36.7 us (11%)
  between operations  13.8 us (4%)
  other arithmetic  5.43 us (2%)
    psum x1, waiting for transfers between devices, local(): gate, upward, hid_grad = lax.psum((gate_part, up_part, grad_part), 'row')  117 us
    reduce_scatter x1, waiting for transfers between devices, local(): lax.psum_scatter(contract(gate_grad, gate_weight, 1, 1) + contract(up_gra...  68.2 us
    all_gather x1, waiting for transfers between devices, local(): lax.all_gather(tokens, 'col', axis=0, tiled=True)  48.1 us
    all_gather x1, waiting for transfers between devices, local(): lax.all_gather(out_grad, 'col', axis=0, tiled=True)  35.8 us
    dot_general x6, matrix products, contract(): lax.dot_general(left, right, (((left_dim,), (right_dim,)), ((), ())), pre...  27 us
  transfers between devices with their start and end apart: 4, of which 4 were waited for; matrix products, arithmetic and copies ran while one was open for 7% of the time, Pallas kernels for 0%

commit v1 on v0

--- a/solution.py
+++ b/solution.py
@@ -3,6 +3,13 @@
 import jax.numpy as jnp
 from jax import lax
 from jax.sharding import PartitionSpec as P
+
+
+def all_by_exchange(x, name, along):
+    size = lax.axis_size(name)
+    parts = jnp.stack([x for _ in range(size)])
+    parts = lax.all_to_all(parts, name, split_axis=0, concat_axis=0)
+    return jnp.concatenate(parts, axis=along)
 
 
 def contract(left, right, left_dim, right_dim):
@@ -23,7 +30,7 @@
 def local(tokens, out_grad, gate_weight, up_weight, down_weight):
     panel_tokens, panel_grads = (
         lax.all_gather(tokens, "col", axis=0, tiled=True),
-        lax.all_gather(out_grad, "col", axis=0, tiled=True),
+        all_by_exchange(out_grad, "col", 0),
     )
     factor = 1.0 / math.sqrt(panel_tokens.shape[0])
     gate_part = jnp.dot(panel_tokens, gate_weight, preferred_element_type=jnp.float32)

time: 327 us -> 294 us (0.90)
  waiting for transfers between devices: 270 us -> 200 us
  blocking collectives: 0 us -> 38.1 us
    all_to_all x0 -> x1, blocking collectives: none -> 38.1 us  [all_by_exchange(): parts = lax.all_to_all(parts, name, split_axis=0, concat_axis=0)]
    all_gather x1 -> x0, waiting for transfers between devices: 35.8 us -> none  [local(): lax.all_gather(out_grad, 'col', axis=0, tiled=True)]
    all_gather x1, waiting for transfers between devices: 48.1 us -> 14.1 us  [local(): lax.all_gather(tokens, 'col', axis=0, tiled=True)]
  transfers between devices with their start and end apart: 4 -> 3, of which waited for: 4 -> 3; matrix products, arithmetic and copies ran while one was open for 7% -> 6% of each run, Pallas kernels for 0% -> 0%
where the time goes in v1:
time: 294 us
  waiting for transfers between devices  200 us (68%)
  blocking collectives  38.1 us (13%)
  matrix products  34 us (12%)
  between operations  13.8 us (5%)
  other arithmetic  5.43 us (2%)
    psum x1, waiting for transfers between devices, local(): gate, upward, hid_grad = lax.psum((gate_part, up_part, grad_part), 'row')  117 us
    reduce_scatter x1, waiting for transfers between devices, local(): lax.psum_scatter(contract(gate_grad, gate_weight, 1, 1) + contract(up_gra...  68.2 us
    all_to_all x1, blocking collectives, all_by_exchange(): parts = lax.all_to_all(parts, name, split_axis=0, concat_axis=0)  38.1 us
    dot_general x6, matrix products, contract(): lax.dot_general(left, right, (((left_dim,), (right_dim,)), ((), ())), pre...  24.3 us
    all_gather x1, waiting for transfers between devices, local(): lax.all_gather(tokens, 'col', axis=0, tiled=True)  14.1 us
    dot_general x1, matrix products, local(): jnp.dot(panel_tokens, up_weight, preferred_element_type=jnp.float32)  6.27 us
  transfers between devices with their start and end apart: 3, of which 3 were waited for; matrix products, arithmetic and copies ran while one was open for 6% of the time, Pallas kernels for 0%

profile of v1, /device:TPU:0, one launch (start us, length us, event | category | flops | bytes accessed | tf_op | source)
XLA Modules:
  0.0 293.8 jit_solution(18366072808431886036)
XLA Ops:
  7.2 0.0 all-gather.2.cloned.1.call-start
  7.2 0.7 all-gather.2.cloned.1.call-update
  7.9 0.0 all-reduce.3.cloned.1.call-start
  7.9 1.1 stack.2
  9.0 0.0 copy-start.7
  9.0 38.1 %all_to_all.5 = bf16[32,16,2048]{2,1,0:T(8,128)(2,1)S(1)} all-to-all(bf16[32,16,2048]{2,1,0:T(8,128)(2,1)S(1)} %stack.2), channel_id=1, replica_groups=mesh['row'=4,'col'=32] {'col'}, dimensions={0} | all-to-all | bytes 4194304 | tf_op jit(solution)/shard_map/all_to_all | solution.py:11
  47.2 1.3 copy-done.3
  48.5 0.0 copy-done.7
  48.5 3.4 %fusion.5 = f32[512,924]{0,1:T(8,128)} fusion(bf16[512,2048]{1,0:T(8,128)(2,1)S(1)} %bitcast.20, bf16[924,2048]{1,0:T(8,128)(2,1)S(1)} %copy-done.7), kind=kOutput, calls=%fused_computation.12 | convolution fusion | flops 1937768448 | bytes 7774208 | tf_op jit(solution)/shard_map/dot_general | solution.py:16
  51.9 14.1 %all-gather.2.cloned.1.call-done = bf16[512,2048]{1,0:T(8,128)(2,1)} async-done(((bf16[16,2048]{1,0:T(8,128)(2,1)}), bf16[512,2048]{1,0:T(8,128)(2,1)}) %all-gather.2.cloned.1.call-update) | async-done | bytes 2097168 | tf_op jit(solution)/shard_map/all_gather | solution.py:32
  66.0 6.3 %fusion.6 = f32[512,924]{0,1:T(8,128)} fusion(bf16[512,2048]{1,0:T(8,128)(2,1)} %all-gather.2.cloned.1.call-done, bf16[2048,924]{0,1:T(8,128)(2,1)} %param.8), kind=kOutput, calls=%fused_computation.13 | convolution fusion | flops 1937768448 | bytes 7774208 | tf_op jit(solution)/shard_map/dot_general | solution.py:37
  72.2 0.0 copy-done
  72.2 0.0 copy-done.8
  72.2 3.4 %fusion.7 = f32[512,924]{0,1:T(8,128)} fusion(bf16[512,2048]{1,0:T(8,128)(2,1)S(1)} %copy-done.8, bf16[2048,924]{0,1:T(8,128)(2,1)S(1)} %copy-done), kind=kOutput, calls=%fused_computation.14 | convolution fusion | flops 1937768448 | bytes 7774208 | tf_op jit(solution)/shard_map/dot_general | solution.py:36
  75.6 0.0 all-reduce.3.cloned.1.call-update
  75.7 0.2 reduce-scatter.2.cloned.1.call-start
  75.9 116.8 %all-reduce.3.cloned.1.call-done = (f32[512,924]{0,1:T(8,128)}, f32[512,924]{0,1:T(8,128)}, f32[512,924]{0,1:T(8,128)}) async-done(((f32[512,924]{0,1:T(8,128)}, f32[512,924]{0,1:T(8,128)}, f32[512,924]{0,1:T(8,128)}), (f32[512,924]{0,1:T(8,128)}, f32[512,924]{0,1:T(8,128)}, f32[512,924]{0,1:T(8,128)})) %all-reduce.3.cloned.1.call-update) | async-done | bytes 5677072 | tf_op jit(solution)/shard_map/psum | solution.py:39
  192.7 3.9 %multiply_convert_fusion.4 = (bf16[512,924]{0,1:T(8,128)(2,1)S(1)}, bf16[512,924]{0,1:T(8,128)(2,1)S(1)}) fusion(f32[512,924]{0,1:T(8,128)} %get-tuple-element.5, f32[512,924]{0,1:T(8,128)} %get-tuple-element.4, f32[512,924]{0,1:T(8,128)} %get-tuple-element.6), kind=kLoop, calls=%fused_computation.7 | loop fusion | flops 6150144 | bytes 7569408 | tf_op jit(solution)/shard_map/convert_element_type | solution.py:26
  196.6 0.0 copy-done.1
  196.6 0.0 copy-start.2
  196.6 2.4 fusion.8
  199.0 0.0 copy-done.2
  199.0 4.5 %convolution_add_fusion = f32[512,2048]{1,0:T(8,128)} fusion(f32[512,2048]{1,0:T(8,128)S(1)} %fusion.8, bf16[512,924]{0,1:T(8,128)(2,1)S(1)} %get-tuple-element.7, bf16[2048,924]{0,1:T(8,128)(2,1)S(1)} %copy-done.2), kind=kOutput, calls=%fused_computation.5 | convolution fusion | flops 1938817024 | bytes 13119488 | tf_op jit(solution)/shard_map/dot_general | solution.py:16
  203.6 0.0 reduce-scatter.2.cloned.1.call-update
  203.6 0.0 copy-start.9
  203.6 5.8 %fusion = bf16[2048,924]{0,1:T(8,128)(2,1)} fusion(bf16[512,924]{0,1:T(8,128)(2,1)S(1)} %get-tuple-element.8, bf16[512,2048]{1,0:T(8,128)(2,1)} %all-gather.2.cloned.1.call-done), kind=kOutput, calls=%fused_computation.3 | convolution fusion | flops 1941553152 | bytes 6828032 | tf_op jit(solution)/shard_map/dot_general | solution.py:16
  209.3 0.0 copy-done.9
  209.4 4.1 %fusion.1 = bf16[2048,924]{0,1:T(8,128)(2,1)} fusion(bf16[512,924]{0,1:T(8,128)(2,1)S(1)} %get-tuple-element.7, bf16[512,2048]{1,0:T(8,128)(2,1)S(1)} %copy-done.9), kind=kOutput, calls=%fused_computation.4 | convolution fusion | flops 1941553152 | bytes 6828032 | tf_op jit(solution)/shard_map/dot_general | solution.py:16
  213.4 0.0 copy-done.5
  213.4 4.1 %multiply_convert_fusion = bf16[924,2048]{1,0:T(8,128)(2,1)} fusion(bf16[512,2048]{1,0:T(8,128)(2,1)S(1)} %bitcast.21, f32[512,924]{0,1:T(8,128)S(1)} %copy-done.6, f32[512,924]{0,1:T(8,128)S(1)} %copy-done.5), kind=kOutput, calls=%fused_computation | convolution fusion | flops 1944391680 | bytes 9666560 | tf_op jit(solution)/shard_map/dot_general | solution.py:16
  217.5 68.2 %reduce-scatter.2.cloned.1.call-done = f32[16,2048]{1,0:T(8,128)} async-done(((f32[512,2048]{1,0:T(8,128)}), f32[16,2048]{1,0:T(8,128)}) %reduce-scatter.2.cloned.1.call-update) | async-done | bytes 131088 | tf_op jit(solution)/shard_map/reduce_scatter | solution.py:41
  285.8 1.5 convert_element_type.29
  (9 shorter events, 0.0 us)
Async XLA Ops:
  7.2 58.8 %all-gather.2.cloned.1.call-start = ((), (), s32[]{:S(2)}) async-start(), calls=%async_computation.2 | async-start | bytes 2162688 | tf_op jit(solution)/shard_map/all_gather | solution.py:32
  7.9 184.8 %all-reduce.3.cloned.1.call-start = ((), (), s32[]{:S(2)}) async-start(), calls=%async_computation.4 | async-start | bytes 11403264 | tf_op jit(solution)/shard_map/psum | solution.py:39
  9.0 39.4 %copy-start.7 = (bf16[924,2048]{1,0:T(8,128)(2,1)S(1)}, bf16[924,2048]{1,0:T(8,128)(2,1)}, u32[]{:S(2)}) copy-start(bf16[924,2048]{1,0:T(8,128)(2,1)} %param.9) | copy-start | bytes 11354116
  47.1 1.3 copy-start.3
  66.0 6.3 %copy-start = (bf16[2048,924]{0,1:T(8,128)(2,1)S(1)}, bf16[2048,924]{0,1:T(8,128)(2,1)}, u32[]{:S(2)}) copy-start(bf16[2048,924]{0,1:T(8,128)(2,1)} %param.7) | copy-start | bytes 11354116
  66.0 6.3 %copy-start.8 = (bf16[512,2048]{1,0:T(8,128)(2,1)S(1)}, bf16[512,2048]{1,0:T(8,128)(2,1)}, u32[]{:S(2)}) copy-start(bf16[512,2048]{1,0:T(8,128)(2,1)} %all-gather.2.cloned.1.call-done) | copy-start | bytes 6291460
  75.7 210.1 %reduce-scatter.2.cloned.1.call-start = ((), (), s32[]{:S(2)}) async-start(), calls=%async_computation.3 | async-start | bytes 4325376 | tf_op jit(solution)/shard_map/reduce_scatter | solution.py:41
  192.7 3.9 %copy-start.1 = (bf16[2048,924]{0,1:T(8,128)(2,1)S(1)}, bf16[2048,924]{0,1:T(8,128)(2,1)}, u32[]{:S(2)}) copy-start(bf16[2048,924]{0,1:T(8,128)(2,1)} %param.7) | copy-start | bytes 11354116
  196.6 2.4 copy-start.2
  203.6 5.8 %copy-start.9 = (bf16[512,2048]{1,0:T(8,128)(2,1)S(1)}, bf16[512,2048]{1,0:T(8,128)(2,1)}, u32[]{:S(2)}) copy-start(bf16[512,2048]{1,0:T(8,128)(2,1)} %all-gather.2.cloned.1.call-done) | copy-start | bytes 6291460
  209.4 4.1 %copy-start.4 = (bf16[32,16,2048]{2,1,0:T(8,128)(2,1)S(1)}, bf16[32,16,2048]{2,1,0:T(8,128)(2,1)}, u32[]{:S(2)}) copy-start(bf16[32,16,2048]{2,1,0:T(8,128)(2,1)} %copy-done.3) | copy-start | bytes 6291460
  209.4 4.1 %copy-start.5 = (f32[512,924]{0,1:T(8,128)S(1)}, f32[512,924]{0,1:T(8,128)}, u32[]{:S(2)}) copy-start(f32[512,924]{0,1:T(8,128)} %get-tuple-element.4) | copy-start | bytes 5677060
  209.4 4.1 %copy-start.6 = (f32[512,924]{0,1:T(8,128)S(1)}, f32[512,924]{0,1:T(8,128)}, u32[]{:S(2)}) copy-start(f32[512,924]{0,1:T(8,128)} %get-tuple-element.6) | copy-start | bytes 5677060
Sparse Core Ops, SparseCore 0:
  10.3 55.6 all-gather.1
  75.8 116.8 all-reduce.2
  203.7 82.0 reduce-scatter.1
